TPU v7x, 256 devices: a whole 4x4x8 slice. The times are simulated.
256 devices in a mesh: dp: 16 (over y, x_hi, core), tensor: 16 (over z, x_lo).
Axes of the slice: x: 4 (x_hi: 2, x_lo: 2; x = x_hi * 2 + x_lo), y: 4, z: 8, core: 2. Of those that a mesh axis runs over, the one named last changes fastest.
Arguments:
- width_side: bfloat16 [16, 2048, 1024], P(None, 'dp'), may hold values from -6 to 6
- hidden_side: bfloat16 [16, 2048, 12288], P(None, 'dp', 'tensor'), may hold values from -0.125 to 0.125
- block_owner: int32 [16], replicated, may hold values from 0 to 15, as said below
- basis_hidden: bfloat16 [16, 2, 12288, 768], P('dp', None, 'tensor'), may hold values from -0.21875 to 0.21875
- basis_width: bfloat16 [16, 2, 1024, 1024], P('dp', None, 'tensor'), may hold values from -0.1875 to 0.1875
- values_hidden: bfloat16 [16, 2, 12288], P('dp', None, 'tensor'), may hold values from 0.29882812 to 3
- values_width: bfloat16 [16, 2, 1024], P('dp'), may hold values from 0.29882812 to 3
Outputs:
- preconditioned: bfloat16 [16, 12288, 1024], P(None, ('tensor', 'dp'))
Inputs may be any that keep to these rules, and one draw needn't show every extreme that they name: `block_owner`: no owner holds more than 2 blocks, and some owner holds exactly 2.
All inputs are finite; a program needn't handle non-finite values.
Results may differ from a plain program's by a relative error of at most 0.023.
Values may be sent and summed in bfloat16 or wider, within the bound.
A program may use at most 256 MiB of HBM per device.

v0:
```python
import jax
import jax.numpy as jnp
from jax import lax
from jax.sharding import PartitionSpec as P

damping_term = 0.1


def slot_ranks(block_owner):
    count_blocks = block_owner.shape[0]
    positions = jnp.arange(count_blocks, dtype=jnp.int32)
    earlier = positions[None, :] < positions[:, None]
    same_owner = block_owner[:, None] == block_owner[None, :]
    return jnp.sum(jnp.logical_and(earlier, same_owner).astype(jnp.int32), axis=1)


def precondition(arrived, hidden_basis, width_basis, hidden_values, width_values):
    sources = arrived.shape[0]
    slots = hidden_basis.shape[0]
    slab_rows = arrived.shape[2]
    basis_split = hidden_basis.reshape(slots, sources, slab_rows, hidden_basis.shape[2])
    left = jnp.einsum(
        "csri,scrw->ciw", basis_split, arrived, preferred_element_type=jnp.float32
    ).astype(jnp.bfloat16)
    middle = jnp.einsum("ciw,cwv->civ", left, width_basis, preferred_element_type=jnp.float32)
    divisor = (
        hidden_values.astype(jnp.float32)[:, :, None] * width_values.astype(jnp.float32)[:, None, :]
        + damping_term
    )
    scaled = (middle / divisor).astype(jnp.bfloat16)
    turned = jnp.einsum(
        "csri,civ->scrv", basis_split, scaled, preferred_element_type=jnp.float32
    ).astype(jnp.bfloat16)
    return jnp.einsum(
        "scrv,cwv->scrw", turned, width_basis, preferred_element_type=jnp.float32
    ).astype(jnp.bfloat16)


def body(
    width_side, hidden_side, block_owner, basis_hidden, basis_width, values_hidden, values_width
):
    dp_count = lax.axis_size("dp")
    grad_rows = lax.psum_scatter(
        jnp.einsum(
            "btf,btw->fbw", hidden_side, width_side, preferred_element_type=jnp.float32
        ).astype(jnp.bfloat16),
        "dp",
        scatter_dimension=0,
        tiled=True,
    )
    ranks = slot_ranks(block_owner)
    slots = basis_hidden.shape[1]
    owner_ids = jnp.arange(dp_count, dtype=jnp.int32)
    slot_ids = jnp.arange(slots, dtype=jnp.int32)
    select = jnp.logical_and(
        block_owner[None, None, :] == owner_ids[:, None, None],
        ranks[None, None, :] == slot_ids[None, :, None],
    ).astype(jnp.bfloat16)
    outgoing = jnp.einsum(
        "ocb,fbw->ocfw", select, grad_rows, preferred_element_type=jnp.float32
    ).astype(jnp.bfloat16)
    arrived = lax.all_to_all(outgoing, "dp", split_axis=0, concat_axis=0, tiled=True)
    width_basis = lax.all_gather(basis_width[0], "tensor", axis=1, tiled=True)
    result = precondition(arrived, basis_hidden[0], width_basis, values_hidden[0], values_width[0])
    returned = lax.all_to_all(result, "dp", split_axis=0, concat_axis=0, tiled=True)
    mine = jnp.einsum("ocb,ocrw->brw", select, returned, preferred_element_type=jnp.float32).astype(
        jnp.bfloat16
    )
    return mine


def solution(mesh):
    return jax.shard_map(
        body,
        mesh=mesh,
        in_specs=(
            P(None, "dp", None),
            P(None, "dp", "tensor"),
            P(),
            P("dp", None, "tensor", None),
            P("dp", None, "tensor", None),
            P("dp", None, "tensor"),
            P("dp", None, None),
        ),
        out_specs=P(None, ("tensor", "dp"), None),
        check_vma=False,
    )
```

profile of v0, /device:TPU:1, one launch (start us, length us, event | category | flops | bytes accessed | tf_op | source)
XLA Modules:
  0.0 418.4 jit_solution(16577890880937635166)
XLA Ops:
  7.4 0.0 copy-start
  7.4 0.0 reduce-scatter.2.cloned.1.call-start
  7.4 1.9 copy-done
  9.3 13.9 %convert_bitcast_fusion = bf16[768,16,1024]{0,2,1:T(8,128)(2,1)} fusion(bf16[16,128,1024]{2,1,0:T(8,128)(2,1)} %param.7, bf16[16,128,768]{2,1,0:T(8,128)(2,1)S(1)} %copy-done), kind=kOutput, calls=%fused_computation | convolution fusion | flops 3233808384 | bytes 32505856 | tf_op jit(solution)/shard_map/btf,btw->fbw/dot_general | solution.py:44
  23.1 32.5 %copy.21 = bf16[768,16,1024]{2,1,0:T(8,128)(2,1)} copy(bf16[768,16,1024]{0,2,1:T(8,128)(2,1)} %convert_bitcast_fusion) | data formatting | bytes 50331648 | tf_op jit(solution)/shard_map/convert_element_type | solution.py:46
  55.6 0.0 copy-start.4
  55.7 0.0 reduce-scatter.2.cloned.1.call-update
  55.7 0.0 all-gather.3.cloned.1.call-start
  55.7 0.5 all-gather.3.cloned.1.call-update
  56.3 0.0 copy-done.4
  56.3 0.1 convert_reduce_fusion
  56.4 0.1 iota_compare_fusion.1
  56.5 230.1 %reduce-scatter.2.cloned.1.call-done = bf16[48,16,1024]{2,1,0:T(8,128)(2,1)} async-done(((bf16[768,16,1024]{2,1,0:T(8,128)(2,1)}), bf16[48,16,1024]{2,1,0:T(8,128)(2,1)}) %reduce-scatter.2.cloned.1.call-update) | async-done | bytes 1572880 | tf_op jit(solution)/shard_map/reduce_scatter | solution.py:43
  286.6 2.8 convolution_convert_fusion
  289.4 3.4 copy.23
  292.7 0.0 copy-start.3
  292.7 0.0 copy-start.2
  292.7 4.9 %all-to-all-start = ((bf16[16,2,48,1024]{3,2,1,0:T(8,128)(2,1)}), bf16[16,2,48,1024]{3,2,1,0:T(8,128)(2,1)S(1)}, u32[]{:S(2)}, u32[]{:S(2)}) async-start(bf16[16,2,48,1024]{3,2,1,0:T(8,128)(2,1)} %copy.23), calls=%async_computation.1 | async-start | bytes 6291456 | tf_op jit(solution)/shard_map/all_to_all | solution.py:62
  297.6 0.0 copy-done.3
  297.6 0.0 copy-done.2
  297.7 0.0 all-gather.3.cloned.1.call-done
  297.7 39.8 %all-to-all-done = bf16[16,2,48,1024]{3,2,1,0:T(8,128)(2,1)S(1)} async-done(((bf16[16,2,48,1024]{3,2,1,0:T(8,128)(2,1)}), bf16[16,2,48,1024]{3,2,1,0:T(8,128)(2,1)S(1)}, u32[]{:S(2)}, u32[]{:S(2)}) %all-to-all-start) | async-done | bytes 3145760 | tf_op jit(solution)/shard_map/all_to_all | solution.py:62
  337.5 11.8 %fusion.2 = f32[2,768,1024]{2,1,0:T(8,128)} fusion(bf16[1,2,1024,1024]{3,2,1,0:T(8,128)(2,1)} %all-gather.3.cloned.1.call-done, bf16[16,2,48,1024]{3,2,1,0:T(8,128)(2,1)S(1)} %all-to-all-done, bf16[2,16,48,768]{3,2,1,0:T(8,128)(2,1)} %bitcast.58), kind=kOutput, calls=%fused_computation.5 | convolution fusion | flops 5638717440 | bytes 15990784 | tf_op jit(solution)/shard_map/ciw,cwv->civ/dot_general | solution.py:25
  349.3 10.8 %convert_bitcast_fusion.1 = bf16[16,2,48,1024]{3,2,0,1:T(8,128)(2,1)S(1)} fusion(bf16[1,2,1024,1024]{3,2,1,0:T(8,128)(2,1)} %all-gather.3.cloned.1.call-done, bf16[2,16,48,768]{3,2,1,0:T(8,128)(2,1)} %bitcast.59, f32[2,768,1024]{2,1,0:T(8,128)} %fusion.2, f32[2,1024]{1,0:T(2,128)S(1)} %bitcast_convert_fusion.3, f32[2,768]{1,0:T(2,128)S(1)} %bitcast_convert_fusion.4), kind=kOutput, calls=%fused_computation.13 | convolution fusion | flops 5646581760 | bytes 16005120 | tf_op jit(solution)/shard_map/scrv,cwv->scrw/dot_general | solution.py:34
  360.1 3.5 copy.27
  363.6 0.0 copy-start.1
  363.6 43.4 %all_to_all.10 = bf16[16,2,48,1024]{3,1,2,0:T(2,128)(2,1)S(1)} all-to-all(bf16[16,2,48,1024]{3,1,2,0:T(2,128)(2,1)S(1)} %copy.27), channel_id=1, replica_groups=mesh['dp'=16,'tensor'=16] {'dp'}, dimensions={0} | all-to-all | bytes 6291456 | tf_op jit(solution)/shard_map/all_to_all | solution.py:65
  407.0 1.9 bitcast_convert_fusion.2
  408.9 2.0 copy.29
  410.9 0.0 copy-done.1
  (3 shorter events, 0.0 us)
Async XLA Ops:
  7.4 1.9 copy-start
  7.4 279.2 %reduce-scatter.2.cloned.1.call-start = ((), (), s32[]{:S(2)}) async-start(), calls=%async_computation.3 | async-start | bytes 26738688 | tf_op jit(solution)/shard_map/reduce_scatter | solution.py:43
  55.6 0.7 copy-start.4
  55.7 242.0 %all-gather.3.cloned.1.call-start = ((), (), s32[]{:S(2)}) async-start(), calls=%async_computation.4 | async-start | bytes 4456448 | tf_op jit(solution)/shard_map/all_gather | solution.py:63
  292.7 4.9 %copy-start.3 = (bf16[1,2,768]{2,1,0:T(2,128)(2,1)S(1)}, bf16[1,2,768]{2,1,0:T(2,128)(2,1)}, u32[]{:S(2)}) copy-start(bf16[1,2,768]{2,1,0:T(2,128)(2,1)} %param.12) | copy-start | bytes 9220
  292.7 4.9 %copy-start.2 = (bf16[1,2,1024]{2,1,0:T(2,128)(2,1)S(1)}, bf16[1,2,1024]{2,1,0:T(2,128)(2,1)}, u32[]{:S(2)}) copy-start(bf16[1,2,1024]{2,1,0:T(2,128)(2,1)} %param.13) | copy-start | bytes 12292
  292.7 44.7 %all-to-all-start = ((bf16[16,2,48,1024]{3,2,1,0:T(8,128)(2,1)}), bf16[16,2,48,1024]{3,2,1,0:T(8,128)(2,1)S(1)}, u32[]{:S(2)}, u32[]{:S(2)}) async-start(bf16[16,2,48,1024]{3,2,1,0:T(8,128)(2,1)} %copy.23), calls=%async_computation.1 | async-start | bytes 6291456 | tf_op jit(solution)/shard_map/all_to_all | solution.py:62
  363.6 47.3 %copy-start.1 = (bf16[16,128,768]{2,1,0:T(8,128)(2,1)S(1)}, bf16[16,128,768]{2,1,0:T(8,128)(2,1)}, u32[]{:S(2)}) copy-start(bf16[16,128,768]{2,1,0:T(8,128)(2,1)} %param.8) | copy-start | bytes 9437188
Sparse Core Ops, SparseCore 0:
  55.8 230.7 reduce-scatter.1
Sparse Core Ops, SparseCore 1:
  57.9 152.3 all-gather.2
where the time goes:
time: 419 us; the launch traced here: 418 us
  waiting for transfers between devices  270 us (64%)
  blocking collectives  43.4 us (10%)
  local copies, waits for them, and re-layouts  43.3 us (10%)
  matrix products  41.2 us (10%)
  between operations  14.9 us (4%)
  starting transfers between devices  4.94 us (1%)
    reduce_scatter x1, waiting for transfers between devices, body(): lax.psum_scatter(jnp.einsum('btf,btw->fbw', hidden_side, width_side, pref...  230 us
    all_to_all x1, blocking collectives, body(): lax.all_to_all(result, 'dp', split_axis=0, concat_axis=0, tiled=True)  43.4 us
    all_to_all x1, waiting for transfers between devices, body(): lax.all_to_all(outgoing, 'dp', split_axis=0, concat_axis=0, tiled=True)  39.8 us
    convert_element_type x1, local copies, waits for them, and re-layouts, body(): grad_rows = lax.psum_scatter(jnp.einsum('btf,btw->fbw', hidden_side, widt...  32.5 us
    dot_general x1, matrix products, body(): jnp.einsum('btf,btw->fbw', hidden_side, width_side, preferred_element_typ...  13.9 us
    dot_general x1, matrix products, precondition(): jnp.einsum('ciw,cwv->civ', left, width_basis, preferred_element_type=jnp....  11.8 us
    dot_general x1, matrix products, precondition(): jnp.einsum('scrv,cwv->scrw', turned, width_basis, preferred_element_type=...  10.8 us
  transfers between devices with their start and end apart: 3, of which 2 were waited for; matrix products, arithmetic and copies ran while one was open for 2% of the time, Pallas kernels for 0%

commit v1 on v0

v1 whole, which is shorter than its diff:
```python
import functools

import jax
import jax.numpy as jnp
from jax import lax
from jax.experimental import pallas as pl
from jax.experimental.pallas import tpu as pltpu
from jax.sharding import PartitionSpec as P

MESH = pl.DeviceIdType.MESH
F32 = jnp.float32
BF16 = jnp.bfloat16

N = 16
NZ = 8
TOK = 128
ROWS = 768
BW = 1024
SLAB = ROWS // N
PIECE = TOK // NZ

SIG, SRC, INV, IDLE = 0, 16, 32, 48
WID, QW1, VAL, QH1, HID, QW2, QH2, OUT = range(8)

damping_term = 0.1


def assignment(block_owner):
    ids = jnp.arange(N, dtype=jnp.int32)
    earlier = ids[None, :] < ids[:, None]
    same = block_owner[:, None] == block_owner[None, :]
    slot = jnp.sum(jnp.logical_and(earlier, same).astype(jnp.int32), axis=1)
    owns = block_owner[None, :] == ids[:, None]
    idle = jnp.logical_not(jnp.any(owns, axis=1))
    over = slot > 0
    idle_rank = jnp.sum(jnp.logical_and(earlier, idle[None, :]).astype(jnp.int32), axis=1)
    over_rank = jnp.sum(jnp.logical_and(earlier, over[None, :]).astype(jnp.int32), axis=1)
    at_owner = jnp.logical_and(owns, jnp.logical_not(over)[None, :])
    moved = jnp.logical_and(
        jnp.logical_and(idle[:, None], over[None, :]), idle_rank[:, None] == over_rank[None, :]
    )
    place = jnp.logical_or(at_owner, moved).astype(jnp.int32)
    sig = jnp.sum(place * ids[None, :], axis=1)
    src = jnp.sum(place * block_owner[None, :], axis=1)
    inv = jnp.sum(place * ids[:, None], axis=0)
    return jnp.concatenate([sig, src, inv, idle.astype(jnp.int32)])


def kernel(
    tbl,
    vals,
    hid,
    wid,
    qh,
    qw,
    out,
    hloc,
    wloc,
    hsend,
    wsend,
    H,
    W,
    WT,
    qw1,
    qw2send,
    qw2,
    qwown,
    Qw,
    QwT,
    vrecv,
    qh1,
    qh2send,
    Q,
    GT,
    LT,
    DT,
    S,
    res,
    R,
    send,
    recv,
    wsem_s,
    wsem_r,
    qsem_s,
    qsem_r,
    xsem,
    loc,
):
    me = lax.axis_index("dp")
    t = lax.axis_index("tensor")
    z, xl = t // 2, t % 2
    up = lax.rem(z + 1, NZ) * 2 + xl
    down = lax.rem(z + NZ - 1, NZ) * 2 + xl
    side = z * 2 + (1 - xl)

    def peer(k):
        y = lax.rem(me // 4 + k // 4, 4)
        x = lax.rem((me // 2) % 2 + (k // 2) % 2, 2)
        c = lax.rem(me % 2 + k % 2, 2)
        return y * 4 + x * 2 + c

    def each_peer(f):
        lax.fori_loop(1, N, lambda k, _: (f(peer(k)), None)[1], None)

    def each(n, f):
        lax.fori_loop(0, n, lambda k, _: (f(k), None)[1], None)

    wloc_cp = pltpu.make_async_copy(wid.at[:, pl.ds(pl.multiple_of(z * PIECE, PIECE), PIECE), :], wloc, loc.at[0])
    wloc_cp.start()
    hloc_cp = pltpu.make_async_copy(hid, hloc, loc.at[1])
    hloc_cp.start()
    own_cp = pltpu.make_async_copy(qh.at[0, 0], Q.at[0], loc.at[2])
    own_cp.start()

    def qw_part(p):
        return qw.at[0, 1, pl.ds(pl.multiple_of((p // 4) * 16, 16), 16), pl.ds(pl.multiple_of((p % 4) * 256, 256), 256)]

    def qh_part(p):
        return qh.at[0, 1, pl.ds(pl.multiple_of(p * SLAB, SLAB), SLAB), :]

    qwown_cp = pltpu.make_async_copy(qw.at[0, 0], qwown, loc.at[3])
    qwown_cp.start()
    qw1_cp = pltpu.make_async_copy(qw_part(me), qw1.at[me], loc.at[4])
    qw1_cp.start()
    qh1_cp = pltpu.make_async_copy(qh_part(me), qh1.at[me], loc.at[5])
    qh1_cp.start()

    barrier = pltpu.get_barrier_semaphore()
    each_peer(lambda p: pl.semaphore_signal(barrier, inc=1, device_id={"dp": p}, device_id_type=MESH))
    for n in (up, down, side):
        pl.semaphore_signal(barrier, inc=1, device_id={"tensor": n}, device_id_type=MESH)
    pl.semaphore_wait(barrier, N + 2)

    def to_peer(kind, src, dst, p):
        return pltpu.make_async_remote_copy(
            src_ref=src,
            dst_ref=dst,
            send_sem=send.at[kind, p],
            recv_sem=recv.at[kind, me],
            device_id={"dp": p},
            device_id_type=MESH,
        )

    def wait_from(kind, dst, p):
        pltpu.make_async_remote_copy(
            src_ref=dst,
            dst_ref=dst,
            send_sem=send.at[kind, p],
            recv_sem=recv.at[kind, p],
            device_id={"dp": p},
            device_id_type=MESH,
        ).wait_recv()

    def wait_sent(kind, src, p):
        pltpu.make_async_remote_copy(
            src_ref=src,
            dst_ref=src,
            send_sem=send.at[kind, p],
            recv_sem=recv.at[kind, p],
            device_id={"dp": p},
            device_id_type=MESH,
        ).wait_send()

    def wrows(p):
        return pl.ds(pl.multiple_of(p * PIECE, PIECE), PIECE)

    vrecv[me] = vals[0]
    wloc_cp.wait()

    def send_first(p):
        wsend[p] = wloc[tbl[SIG + p]]
        to_peer(WID, wsend.at[p], W.at[z, wrows(me), :], p).start()
        to_peer(QW1, qw_part(p), qw1.at[me], p).start()
        to_peer(VAL, vals.at[1], vrecv.at[me], p).start()

    each_peer(send_first)
    W[z, wrows(me), :] = wloc[tbl[SIG + me]]

    each_peer(lambda p: to_peer(QH1, qh_part(p), qh1.at[me], p).start())

    def wpiece(step, way):
        if way == 0:
            piece = lax.rem(z + NZ - step, NZ)
        else:
            piece = lax.rem(z + step, NZ)
        if step < NZ // 2 - 1:
            return W.at[piece]
        half = N * PIECE // 2
        return W.at[piece, pl.ds(way * half, half), :]

    def qpiece(step, way):
        if way == 0:
            piece = lax.rem(z + NZ - step, NZ)
        else:
            piece = lax.rem(z + step, NZ)
        if step < NZ // 2 - 1:
            return Qw.at[piece]
        return Qw.at[piece, pl.ds(way * 64, 64), :]

    def ring(pieces, s, r, step, way):
        part = pieces(step, way)
        return pltpu.make_async_remote_copy(
            src_ref=part,
            dst_ref=part,
            send_sem=s.at[way, step],
            recv_sem=r.at[way, step],
            device_id={"tensor": up if way == 0 else down},
            device_id_type=MESH,
        )

    def landed(pieces, s, r, step, way):
        part = pieces(step, way)
        if way == 0:
            piece = lax.rem(z + NZ - step - 1, NZ)
        else:
            piece = lax.rem(z + step + 1, NZ)
        whole = W if pieces is wpiece else Qw
        if step < NZ // 2 - 1:
            part = whole.at[piece]
        else:
            half = (N * PIECE // 2) if pieces is wpiece else 64
            part = whole.at[piece, pl.ds(way * half, half), :]
        return pltpu.make_async_remote_copy(
            src_ref=part,
            dst_ref=part,
            send_sem=s.at[way, step],
            recv_sem=r.at[way, step],
            device_id={"tensor": up if way == 0 else down},
            device_id_type=MESH,
        )

    def ring_start(pieces, s, r, step):
        for way in range(2):
            ring(pieces, s, r, step, way).start()

    def ring_wait(pieces, s, r, step):
        for way in range(2):
            landed(pieces, s, r, step, way).wait_recv()

    def turn_width(piece):
        def part(n):
            cols = pl.ds(pl.multiple_of(n * 256, 256), 256)
            WT[cols, pl.ds(pl.multiple_of(piece * 256, 256), 256)] = W[piece, :, cols].T

        each(BW // 256, part)

    def turn_basis(piece):
        def part(n):
            cols = pl.ds(pl.multiple_of(n * 256, 256), 256)
            QwT[cols, pl.ds(pl.multiple_of(piece * 128, 128), 128)] = Qw[piece, :, cols].T

        each(BW // 256, part)

    each_peer(lambda p: wait_from(WID, W.at[z, wrows(p), :], p))
    ring_start(wpiece, wsem_s, wsem_r, 0)

    qw1_cp.wait()
    each_peer(lambda p: wait_from(QW1, qw1.at[p], p))

    def qw_place(p):
        return (
            pl.ds(pl.multiple_of((p // 4) * 16, 16), 16),
            pl.ds(pl.multiple_of((p % 4) * 256, 256), 256),
        )

    def send_qw2(p):
        qw2send[p] = qw1[tbl[SRC + p]]
        rows, cols = qw_place(me)
        to_peer(QW2, qw2send.at[p], qw2.at[rows, cols], p).start()

    each_peer(send_qw2)
    own_rows, own_cols = qw_place(me)
    qw2[own_rows, own_cols] = qw1[tbl[SRC + me]]

    hloc_cp.wait()

    def send_hidden(p):
        hsend[p] = hloc[tbl[SIG + p]].reshape(NZ, PIECE, ROWS)
        to_peer(HID, hsend.at[p], H.at[:, me], p).start()

    each_peer(send_hidden)
    H[:, me] = hloc[tbl[SIG + me]].reshape(NZ, PIECE, ROWS)

    qwown_cp.wait()

    def wait_qw2(p):
        rows, cols = qw_place(p)
        wait_from(QW2, qw2.at[rows, cols], p)

    each_peer(wait_qw2)
    idle = tbl[IDLE + me]
    mine = pl.ds(pl.multiple_of(xl * 64, 64), 64)
    theirs = pl.ds(pl.multiple_of((1 - xl) * 64, 64), 64)
    Qw[z, mine, :] = jnp.where(idle > 0, qw2[...], qwown[...])
    swap = pltpu.make_async_remote_copy(
        src_ref=Qw.at[z, mine, :],
        dst_ref=Qw.at[z, mine, :],
        send_sem=xsem.at[0],
        recv_sem=xsem.at[1],
        device_id={"tensor": side},
        device_id_type=MESH,
    )
    swap.start()

    each_peer(lambda p: wait_from(VAL, vrecv.at[p], p))
    v = vrecv[tbl[SRC + me]]
    vt = jnp.concatenate([v, jnp.zeros((120, 256), F32)], axis=0).T
    for c in range(4):
        for r in range(3):
            DT[256 * c : 256 * (c + 1), 256 * r : 256 * (r + 1)] = 1.0 / (
                vt[:, 3 + c : 4 + c] * v[r : r + 1, :] + damping_term
            )

    pltpu.make_async_remote_copy(
        src_ref=Qw.at[z, theirs, :],
        dst_ref=Qw.at[z, theirs, :],
        send_sem=xsem.at[0],
        recv_sem=xsem.at[1],
        device_id={"tensor": side},
        device_id_type=MESH,
    ).wait_recv()
    ring_start(qpiece, qsem_s, qsem_r, 0)
    turn_width(z)
    turn_basis(z)

    def advance(step):
        ring_wait(wpiece, wsem_s, wsem_r, step)
        if step < 3:
            ring_start(wpiece, wsem_s, wsem_r, step + 1)
        ring_wait(qpiece, qsem_s, qsem_r, step)
        if step < 3:
            ring_start(qpiece, qsem_s, qsem_r, step + 1)
        for piece in ((z + NZ - step - 1) % NZ, (z + step + 1) % NZ)[: 2 if step < 3 else 1]:
            turn_width(piece)
            turn_basis(piece)

    advance(0)

    qh1_cp.wait()
    each_peer(lambda p: wait_from(QH1, qh1.at[p], p))

    def slab(p):
        return pl.ds(pl.multiple_of(p * SLAB, SLAB), SLAB)

    def send_qh2(p):
        qh2send[p] = qh1[tbl[SRC + p]]
        to_peer(QH2, qh2send.at[p], Q.at[1, slab(me), :], p).start()

    each_peer(send_qh2)
    Q[1, slab(me), :] = qh1[tbl[SRC + me]]

    advance(1)
    advance(2)
    advance(3)

    each_peer(lambda p: wait_from(HID, H.at[:, p], p))

    def gradient(n):
        rows = pl.ds(pl.multiple_of(n * 256, 256), 256)
        GT[rows, :] = jnp.dot(
            WT[rows, :], H[...].reshape(N * TOK, ROWS), preferred_element_type=F32
        ).astype(BF16)

    each(BW // 256, gradient)

    own_cp.wait()
    each_peer(lambda p: wait_from(QH2, Q.at[1, slab(p), :], p))

    def left(n):
        rows = pl.ds(pl.multiple_of(n * 256, 256), 256)
        LT[rows, :] = jnp.dot(GT[rows, :], Q[idle], preferred_element_type=F32).astype(BF16)

    each(BW // 256, left)

    def middle(n):
        rows = pl.ds(pl.multiple_of(n * 256, 256), 256)
        S[rows, :] = (
            jnp.dot(QwT[rows, :], LT[...], preferred_element_type=F32) * DT[rows, :]
        ).astype(BF16)

    each(BW // 256, middle)

    def finish(n):
        group = lax.rem(me // 4 + 1 + n, 4)
        rows = pl.ds(pl.multiple_of(group * 192, 192), 192)
        turned = lax.dot_general(
            Q[idle, rows, :], S[...], (((1,), (1,)), ((), ())), preferred_element_type=F32
        ).astype(BF16)
        final = jnp.dot(turned, QwT[...], preferred_element_type=F32).astype(BF16)
        res[pl.ds(group * 4, 4)] = final.reshape(4, SLAB, BW)
        for i in range(4):
            q = group * 4 + i

            @pl.when(q != me)
            def _():
                to_peer(OUT, res.at[q], R.at[me], q).start()

    each(4, finish)
    R[me] = res[me]

    each_peer(lambda p: wait_sent(WID, wsend.at[p], p))
    each_peer(lambda p: wait_sent(QW1, qw_part(p), p))
    each_peer(lambda p: wait_sent(VAL, vals.at[1], p))
    each_peer(lambda p: wait_sent(QH1, qh_part(p), p))
    each_peer(lambda p: wait_sent(QW2, qw2send.at[p], p))
    each_peer(lambda p: wait_sent(HID, hsend.at[p], p))
    each_peer(lambda p: wait_sent(QH2, qh2send.at[p], p))
    swap.wait_send()
    for step in range(4):
        for way in range(2):
            ring(wpiece, wsem_s, wsem_r, step, way).wait_send()
            ring(qpiece, qsem_s, qsem_r, step, way).wait_send()

    each_peer(lambda p: wait_from(OUT, R.at[p], p))
    each_peer(lambda p: wait_sent(OUT, res.at[p], p))

    def place(b):
        out[b] = R[tbl[INV + b]]

    each(N, place)


def body(
    width_side, hidden_side, block_owner, basis_hidden, basis_width, values_hidden, values_width
):
    table = assignment(block_owner)
    vals = jnp.concatenate(
        [
            values_hidden[0].astype(F32),
            values_width[0].astype(F32),
            jnp.zeros((2, 256), F32),
        ],
        axis=1,
    ).reshape(2, 8, 256)
    any_spec = pl.BlockSpec(memory_space=pl.ANY)
    vmem_spec = pl.BlockSpec(memory_space=pltpu.VMEM)
    dma = pltpu.SemaphoreType.DMA
    return pl.pallas_call(
        kernel,
        out_shape=jax.ShapeDtypeStruct((N, SLAB, BW), BF16),
        in_specs=[pl.BlockSpec(memory_space=pltpu.SMEM), vmem_spec] + [any_spec] * 4,
        out_specs=vmem_spec,
        scratch_shapes=[
            pltpu.VMEM((N, TOK, ROWS), BF16),
            pltpu.VMEM((N, PIECE, BW), BF16),
            pltpu.VMEM((N, NZ, PIECE, ROWS), BF16),
            pltpu.VMEM((N, PIECE, BW), BF16),
            pltpu.VMEM((NZ, N, PIECE, ROWS), BF16),
            pltpu.VMEM((NZ, N * PIECE, BW), BF16),
            pltpu.VMEM((BW, N * TOK), BF16),
            pltpu.VMEM((N, 16, 256), BF16),
            pltpu.VMEM((N, 16, 256), BF16),
            pltpu.VMEM((64, BW), BF16),
            pltpu.VMEM((64, BW), BF16),
            pltpu.VMEM((NZ, 128, BW), BF16),
            pltpu.VMEM((BW, BW), BF16),
            pltpu.VMEM((N, 8, 256), F32),
            pltpu.VMEM((N, SLAB, ROWS), BF16),
            pltpu.VMEM((N, SLAB, ROWS), BF16),
            pltpu.VMEM((2, ROWS, ROWS), BF16),
            pltpu.VMEM((BW, ROWS), BF16),
            pltpu.VMEM((BW, ROWS), BF16),
            pltpu.VMEM((BW, ROWS), F32),
            pltpu.VMEM((BW, ROWS), BF16),
            pltpu.VMEM((N, SLAB, BW), BF16),
            pltpu.VMEM((N, SLAB, BW), BF16),
            dma((8, N)),
            dma((8, N)),
            dma((2, 4)),
            dma((2, 4)),
            dma((2, 4)),
            dma((2, 4)),
            dma((2,)),
            dma((6,)),
        ],
        compiler_params=pltpu.CompilerParams(
            collective_id=0, has_side_effects=True, vmem_limit_bytes=56 * 2**20
        ),
        cost_estimate=pl.CostEstimate(
            flops=2 * ROWS * BW * (2048 + 2 * ROWS + 2 * BW), bytes_accessed=10 * 2**20, transcendentals=0
        ),
    )(table, vals, hidden_side, width_side, basis_hidden, basis_width)


def solution(mesh):
    return jax.shard_map(
        body,
        mesh=mesh,
        in_specs=(
            P(None, "dp", None),
            P(None, "dp", "tensor"),
            P(),
            P("dp", None, "tensor", None),
            P("dp", None, "tensor", None),
            P("dp", None, "tensor"),
            P("dp", None, None),
        ),
        out_specs=P(None, ("tensor", "dp"), None),
        check_vma=False,
    )
```

time: 419 us -> 166 us (0.40)
  waiting for transfers between devices: 270 us -> 0 us
  Pallas kernels: 0 us -> 158 us
  blocking collectives: 43.4 us -> 0 us
  matrix products: 41.2 us -> 0 us
  local copies, waits for them, and re-layouts: 43.3 us -> 3.33 us
  between operations: 14.9 us -> 0.02 us
  starting transfers between devices: 4.94 us -> 0 us
  other arithmetic: 0.18 us -> 4.68 us
    reduce_scatter x1 -> x0, waiting for transfers between devices: 230 us -> none  [body(): lax.psum_scatter(jnp.einsum('btf,btw->fbw', hidden_side, width_side, pref...]
    pallas_call x0 -> x1, Pallas kernels: none -> 158 us  [body(): pl.pallas_call(kernel, out_shape=jax.ShapeDtypeStruct((N, SLAB, BW), BF16...]
    all_to_all x1 -> x0, blocking collectives: 43.4 us -> none  [body(): lax.all_to_all(result, 'dp', split_axis=0, concat_axis=0, tiled=True)]
    convert_element_type x4 -> x0, local copies, waits for them, and re-layouts: 41.4 us -> none  [the longest x1 32.5 us: body(): grad_rows = lax.psum_scatter(jnp.einsum('btf,btw->fbw', hidden_side, widt...]
    dot_general x5 -> x0, matrix products: 41.2 us -> none  [the longest x1 13.9 us: body(): jnp.einsum('btf,btw->fbw', hidden_side, width_side, preferred_element_typ...]
    all_to_all x1 -> x0, waiting for transfers between devices: 39.8 us -> none  [body(): lax.all_to_all(outgoing, 'dp', split_axis=0, concat_axis=0, tiled=True)]
    all_to_all x1 -> x0, starting transfers between devices: 4.89 us -> none  [body(): lax.all_to_all(outgoing, 'dp', split_axis=0, concat_axis=0, tiled=True)]
  transfers between devices with their start and end apart: 3 -> 0, of which waited for: 2 -> 0; matrix products, arithmetic and copies ran while one was open for 2% -> 0% of each run, Pallas kernels for 0% -> 0%
where the time goes in v1:
time: 166 us
  Pallas kernels  158 us (95%)
  other arithmetic  4.68 us (3%)
  local copies, waits for them, and re-layouts  3.33 us (2%)
    pallas_call x1, Pallas kernels, body(): pl.pallas_call(kernel, out_shape=jax.ShapeDtypeStruct((N, SLAB, BW), BF16...  158 us
    unnamed x2, local copies, waits for them, and re-layouts  3.32 us

profile of v1, /device:TPU:1, one launch (start us, length us, event | category | flops | bytes accessed | tf_op | source)
XLA Modules:
  0.0 166.2 jit_solution(12003841762500934023)
XLA Ops:
  0.0 0.8 fusion.3
  0.8 0.9 convert_reduce_fusion.2
  1.7 0.1 convert_reduce_fusion
  1.8 0.9 select_reduce_fusion.2
  2.7 0.6 pad_add_fusion.tbl
  3.3 0.7 bitcast_convert_fusion.1
  4.0 0.7 bitcast_convert_fusion
  4.7 0.6 copy.10
  5.3 158.2 %shard_map.73 = bf16[16,48,1024]{2,1,0:T(8,128)(2,1)} custom-call(s32[64]{0:T(128)} %pad_add_fusion.tbl, f32[2,8,256]{2,1,0:T(8,128)} %bitcast.11, bf16[16,128,768]{2,1,0:T(8,128)(2,1)} %hid.1, bf16[16,128,1024]{2,1,0:T(8,128)(2,1)} %wid.1, bf16[1,2,768,768]{3,2,1,0:T(8,128)(2,1)} %qh.1, bf16[1,2,64,1024]{3,2,1,0:T(8,128)(2,1)} %qw.1), custom_call_target="tpu_custom_call" | custom-call | flops 8858370048 | bytes 10485760 | tf_op jit(solution)/shard_map/pallas_call | solution.py:438
  163.5 2.7 %copy.12 = bf16[16,48,1024]{2,1,0:T(8,128)(2,1)} copy(bf16[16,48,1024]{2,1,0:T(8,128)(2,1)} %shard_map.73) | data formatting | bytes 3145728
  (5 shorter events, 0.0 us)

commit v2 on v1

--- a/solution.py
+++ b/solution.py
@@ -129,7 +129,9 @@
     each_peer(lambda p: pl.semaphore_signal(barrier, inc=1, device_id={"dp": p}, device_id_type=MESH))
     for n in (up, down, side):
         pl.semaphore_signal(barrier, inc=1, device_id={"tensor": n}, device_id_type=MESH)
+
     pl.semaphore_wait(barrier, N + 2)
+    vrecv[me] = vals[0]
 
     def to_peer(kind, src, dst, p):
         return pltpu.make_async_remote_copy(
@@ -164,19 +166,16 @@
     def wrows(p):
         return pl.ds(pl.multiple_of(p * PIECE, PIECE), PIECE)
 
-    vrecv[me] = vals[0]
+    each_peer(lambda p: to_peer(QW1, qw_part(p), qw1.at[me], p).start())
     wloc_cp.wait()
 
-    def send_first(p):
+    def send_width(p):
         wsend[p] = wloc[tbl[SIG + p]]
         to_peer(WID, wsend.at[p], W.at[z, wrows(me), :], p).start()
-        to_peer(QW1, qw_part(p), qw1.at[me], p).start()
-        to_peer(VAL, vals.at[1], vrecv.at[me], p).start()
-
-    each_peer(send_first)
+
+    each_peer(send_width)
     W[z, wrows(me), :] = wloc[tbl[SIG + me]]
-
-    each_peer(lambda p: to_peer(QH1, qh_part(p), qh1.at[me], p).start())
+    each_peer(lambda p: to_peer(VAL, vals.at[1], vrecv.at[me], p).start())
 
     def wpiece(step, way):
         if way == 0:
@@ -251,18 +250,15 @@
 
         each(BW // 256, part)
 
-    each_peer(lambda p: wait_from(WID, W.at[z, wrows(p), :], p))
-    ring_start(wpiece, wsem_s, wsem_r, 0)
-
-    qw1_cp.wait()
-    each_peer(lambda p: wait_from(QW1, qw1.at[p], p))
-
     def qw_place(p):
         return (
             pl.ds(pl.multiple_of((p // 4) * 16, 16), 16),
             pl.ds(pl.multiple_of((p % 4) * 256, 256), 256),
         )
 
+    qw1_cp.wait()
+    each_peer(lambda p: wait_from(QW1, qw1.at[p], p))
+
     def send_qw2(p):
         qw2send[p] = qw1[tbl[SRC + p]]
         rows, cols = qw_place(me)
@@ -272,14 +268,10 @@
     own_rows, own_cols = qw_place(me)
     qw2[own_rows, own_cols] = qw1[tbl[SRC + me]]
 
-    hloc_cp.wait()
-
-    def send_hidden(p):
-        hsend[p] = hloc[tbl[SIG + p]].reshape(NZ, PIECE, ROWS)
-        to_peer(HID, hsend.at[p], H.at[:, me], p).start()
-
-    each_peer(send_hidden)
-    H[:, me] = hloc[tbl[SIG + me]].reshape(NZ, PIECE, ROWS)
+    each_peer(lambda p: to_peer(QH1, qh_part(p), qh1.at[me], p).start())
+
+    each_peer(lambda p: wait_from(WID, W.at[z, wrows(p), :], p))
+    ring_start(wpiece, wsem_s, wsem_r, 0)
 
     qwown_cp.wait()
 
@@ -302,14 +294,14 @@
     )
     swap.start()
 
-    each_peer(lambda p: wait_from(VAL, vrecv.at[p], p))
-    v = vrecv[tbl[SRC + me]]
-    vt = jnp.concatenate([v, jnp.zeros((120, 256), F32)], axis=0).T
-    for c in range(4):
-        for r in range(3):
-            DT[256 * c : 256 * (c + 1), 256 * r : 256 * (r + 1)] = 1.0 / (
-                vt[:, 3 + c : 4 + c] * v[r : r + 1, :] + damping_term
-            )
+    hloc_cp.wait()
+
+    def send_hidden(p):
+        hsend[p] = hloc[tbl[SIG + p]].reshape(NZ, PIECE, ROWS)
+        to_peer(HID, hsend.at[p], H.at[:, me], p).start()
+
+    each_peer(send_hidden)
+    H[:, me] = hloc[tbl[SIG + me]].reshape(NZ, PIECE, ROWS)
 
     pltpu.make_async_remote_copy(
         src_ref=Qw.at[z, theirs, :],
@@ -320,21 +312,35 @@
         device_id_type=MESH,
     ).wait_recv()
     ring_start(qpiece, qsem_s, qsem_r, 0)
+
+    each_peer(lambda p: wait_from(VAL, vrecv.at[p], p))
+    v = vrecv[tbl[SRC + me]]
+    for c in range(8):
+        row, at = 3 + c // 2, 128 * (c % 2)
+        lw = jnp.broadcast_to(v[row : row + 1, at : at + 128], (128, 128)).T
+        for r in range(6):
+            row, at = r // 2, 128 * (r % 2)
+            DT[128 * c : 128 * (c + 1), 128 * r : 128 * (r + 1)] = 1.0 / (
+                lw * v[row : row + 1, at : at + 128] + damping_term
+            )
+
     turn_width(z)
     turn_basis(z)
 
-    def advance(step):
-        ring_wait(wpiece, wsem_s, wsem_r, step)
+    def advance(pieces, s, r, step, turn):
+        ring_wait(pieces, s, r, step)
         if step < 3:
-            ring_start(wpiece, wsem_s, wsem_r, step + 1)
-        ring_wait(qpiece, qsem_s, qsem_r, step)
-        if step < 3:
-            ring_start(qpiece, qsem_s, qsem_r, step + 1)
+            ring_start(pieces, s, r, step + 1)
         for piece in ((z + NZ - step - 1) % NZ, (z + step + 1) % NZ)[: 2 if step < 3 else 1]:
-            turn_width(piece)
-            turn_basis(piece)
-
-    advance(0)
+            turn(piece)
+
+    def advance_w(step):
+        advance(wpiece, wsem_s, wsem_r, step, turn_width)
+
+    def advance_q(step):
+        advance(qpiece, qsem_s, qsem_r, step, turn_basis)
+
+    advance_w(0)
 
     qh1_cp.wait()
     each_peer(lambda p: wait_from(QH1, qh1.at[p], p))
@@ -349,9 +355,12 @@
     each_peer(send_qh2)
     Q[1, slab(me), :] = qh1[tbl[SRC + me]]
 
-    advance(1)
-    advance(2)
-    advance(3)
+    advance_q(0)
+    advance_w(1)
+    advance_q(1)
+    advance_w(2)
+    advance_q(2)
+    advance_w(3)
 
     each_peer(lambda p: wait_from(HID, H.at[:, p], p))
 
@@ -371,6 +380,7 @@
         LT[rows, :] = jnp.dot(GT[rows, :], Q[idle], preferred_element_type=F32).astype(BF16)
 
     each(BW // 256, left)
+    advance_q(3)
 
     def middle(n):
         rows = pl.ds(pl.multiple_of(n * 256, 256), 256)
@@ -413,6 +423,7 @@
 
     each_peer(lambda p: wait_from(OUT, R.at[p], p))
     each_peer(lambda p: wait_sent(OUT, res.at[p], p))
+
 
     def place(b):
         out[b] = R[tbl[INV + b]]
@@ -435,10 +446,11 @@
     any_spec = pl.BlockSpec(memory_space=pl.ANY)
     vmem_spec = pl.BlockSpec(memory_space=pltpu.VMEM)
     dma = pltpu.SemaphoreType.DMA
+    smem_spec = pl.BlockSpec(memory_space=pltpu.SMEM)
     return pl.pallas_call(
         kernel,
         out_shape=jax.ShapeDtypeStruct((N, SLAB, BW), BF16),
-        in_specs=[pl.BlockSpec(memory_space=pltpu.SMEM), vmem_spec] + [any_spec] * 4,
+        in_specs=[smem_spec, vmem_spec] + [any_spec] * 4,
         out_specs=vmem_spec,
         scratch_shapes=[
             pltpu.VMEM((N, TOK, ROWS), BF16),
@@ -471,7 +483,7 @@
             dma((2, 4)),
             dma((2, 4)),
             dma((2,)),
-            dma((6,)),
+            dma((7,)),
         ],
         compiler_params=pltpu.CompilerParams(
             collective_id=0, has_side_effects=True, vmem_limit_bytes=56 * 2**20

time: 166 us -> 128 us (0.77)
  Pallas kernels: 158 us -> 120 us
    pallas_call x1, Pallas kernels: 158 us -> 120 us  [body(): pl.pallas_call(kernel, out_shape=jax.ShapeDtypeStruct((N, SLAB, BW), BF16...]
where the time goes in v2:
time: 128 us
  Pallas kernels  120 us (94%)
  other arithmetic  4.68 us (4%)
  local copies, waits for them, and re-layouts  3.33 us (3%)
    pallas_call x1, Pallas kernels, body(): pl.pallas_call(kernel, out_shape=jax.ShapeDtypeStruct((N, SLAB, BW), BF16...  120 us
    unnamed x2, local copies, waits for them, and re-layouts  3.32 us

profile of v2, /device:TPU:1, one launch (start us, length us, event | category | flops | bytes accessed | tf_op | source)
XLA Modules:
  0.0 128.0 jit_solution(5671920030852584802)
XLA Ops:
  0.0 0.8 fusion.3
  0.8 0.9 convert_reduce_fusion.2
  1.7 0.1 convert_reduce_fusion
  1.8 0.9 select_reduce_fusion.2
  2.7 0.6 pad_add_fusion.tbl
  3.3 0.7 bitcast_convert_fusion.1
  4.0 0.7 bitcast_convert_fusion
  4.7 0.6 copy.10
  5.3 120.0 %shard_map.73 = bf16[16,48,1024]{2,1,0:T(8,128)(2,1)} custom-call(s32[64]{0:T(128)} %pad_add_fusion.tbl, f32[2,8,256]{2,1,0:T(8,128)} %bitcast.11, bf16[16,128,768]{2,1,0:T(8,128)(2,1)} %hid.1, bf16[16,128,1024]{2,1,0:T(8,128)(2,1)} %wid.1, bf16[1,2,768,768]{3,2,1,0:T(8,128)(2,1)} %qh.1, bf16[1,2,64,1024]{3,2,1,0:T(8,128)(2,1)} %qw.1), custom_call_target="tpu_custom_call" | custom-call | flops 8858370048 | bytes 10485760 | tf_op jit(solution)/shard_map/pallas_call | solution.py:450
  125.3 2.7 %copy.12 = bf16[16,48,1024]{2,1,0:T(8,128)(2,1)} copy(bf16[16,48,1024]{2,1,0:T(8,128)(2,1)} %shard_map.73) | data formatting | bytes 3145728
  (5 shorter events, 0.0 us)

commit v3 on v2

--- a/solution.py
+++ b/solution.py
@@ -19,31 +19,63 @@
 SLAB = ROWS // N
 PIECE = TOK // NZ
 
-SIG, SRC, INV, IDLE = 0, 16, 32, 48
+SIG, SRC, INV, IDLE = range(4)
 WID, QW1, VAL, QH1, HID, QW2, QH2, OUT = range(8)
 
 damping_term = 0.1
 
 
-def assignment(block_owner):
-    ids = jnp.arange(N, dtype=jnp.int32)
-    earlier = ids[None, :] < ids[:, None]
-    same = block_owner[:, None] == block_owner[None, :]
-    slot = jnp.sum(jnp.logical_and(earlier, same).astype(jnp.int32), axis=1)
-    owns = block_owner[None, :] == ids[:, None]
-    idle = jnp.logical_not(jnp.any(owns, axis=1))
-    over = slot > 0
-    idle_rank = jnp.sum(jnp.logical_and(earlier, idle[None, :]).astype(jnp.int32), axis=1)
-    over_rank = jnp.sum(jnp.logical_and(earlier, over[None, :]).astype(jnp.int32), axis=1)
-    at_owner = jnp.logical_and(owns, jnp.logical_not(over)[None, :])
-    moved = jnp.logical_and(
-        jnp.logical_and(idle[:, None], over[None, :]), idle_rank[:, None] == over_rank[None, :]
-    )
-    place = jnp.logical_or(at_owner, moved).astype(jnp.int32)
-    sig = jnp.sum(place * ids[None, :], axis=1)
-    src = jnp.sum(place * block_owner[None, :], axis=1)
-    inv = jnp.sum(place * ids[:, None], axis=0)
-    return jnp.concatenate([sig, src, inv, idle.astype(jnp.int32)])
+def make_table(owner):
+    shape = (N, 128)
+    sub = lax.broadcasted_iota(jnp.int32, shape, 0)
+    lane = lax.broadcasted_iota(jnp.int32, shape, 1)
+    on_lane = jnp.full(shape, -1, jnp.int32)
+    on_sub = jnp.full(shape, -1, jnp.int32)
+    for b in range(N):
+        on_lane = jnp.where(lane == b, owner[b], on_lane)
+        on_sub = jnp.where(sub == b, owner[b], on_sub)
+
+    def count(mask, axis):
+        return jnp.sum(jnp.where(mask, 1, 0), axis=axis, keepdims=True)
+
+    same = on_lane == on_sub
+    over_lane = count(jnp.logical_and(same, sub < lane), 0) > 0
+    over_sub = count(jnp.logical_and(same, lane < sub), 1) > 0
+    idle_lane = jnp.logical_and(count(on_sub == lane, 0) == 0, lane[:1] < N)
+    idle_sub = count(on_lane == sub, 1) == 0
+    over_lane_rank = count(jnp.logical_and(over_sub, sub < lane), 0)
+    over_sub_rank = count(jnp.logical_and(over_lane, lane < sub), 1)
+    idle_lane_rank = count(jnp.logical_and(idle_sub, sub < lane), 0)
+    idle_sub_rank = count(jnp.logical_and(idle_lane, lane < sub), 1)
+
+    def placed(owns, over, idle, over_rank, idle_rank):
+        moved = jnp.logical_and(jnp.logical_and(idle, over), over_rank == idle_rank)
+        return jnp.logical_or(jnp.logical_and(owns, jnp.logical_not(over)), moved)
+
+    here = placed(on_sub == lane, over_sub, idle_lane, over_sub_rank, idle_lane_rank)
+    there = placed(on_lane == sub, over_lane, idle_sub, over_lane_rank, idle_sub_rank)
+    sig = jnp.sum(jnp.where(here, sub, 0), axis=0, keepdims=True)
+    src = jnp.sum(jnp.where(here, on_sub, 0), axis=0, keepdims=True)
+    inv = jnp.sum(jnp.where(there, sub, 0), axis=0, keepdims=True)
+    idle = jnp.where(idle_lane, 1, 0)
+    row = lax.broadcasted_iota(jnp.int32, (8, 128), 0)
+    table = jnp.zeros((8, 128), jnp.int32)
+    for k, part in ((SIG, sig), (SRC, src), (INV, inv), (IDLE, idle)):
+        table = jnp.where(row == k, part, table)
+    return table
+
+
+def prepare(owner, vh, vw, tbl, vals, rows):
+    tbl[...] = make_table(owner)
+    both_h = vh[0].astype(F32)
+    both_w = vw[0].astype(F32)
+    for c in range(2):
+        for r in range(6):
+            rows[c, r : r + 1, :] = both_h[c : c + 1, 128 * r : 128 * (r + 1)]
+        for r in range(8):
+            rows[c, 6 + r : 7 + r, :] = both_w[c : c + 1, 128 * r : 128 * (r + 1)]
+        rows[c, 14:16, :] = jnp.zeros((2, 128), F32)
+    vals[...] = rows[...].astype(BF16)
 
 
 def kernel(
@@ -53,7 +85,7 @@
     wid,
     qh,
     qw,
-    out,
+    R,
     hloc,
     wloc,
     hsend,
@@ -76,7 +108,6 @@
     DT,
     S,
     res,
-    R,
     send,
     recv,
     wsem_s,
@@ -170,11 +201,11 @@
     wloc_cp.wait()
 
     def send_width(p):
-        wsend[p] = wloc[tbl[SIG + p]]
+        wsend[p] = wloc[tbl[SIG, p]]
         to_peer(WID, wsend.at[p], W.at[z, wrows(me), :], p).start()
 
     each_peer(send_width)
-    W[z, wrows(me), :] = wloc[tbl[SIG + me]]
+    W[z, wrows(me), :] = wloc[tbl[SIG, me]]
     each_peer(lambda p: to_peer(VAL, vals.at[1], vrecv.at[me], p).start())
 
     def wpiece(step, way):
@@ -260,13 +291,13 @@
     each_peer(lambda p: wait_from(QW1, qw1.at[p], p))
 
     def send_qw2(p):
-        qw2send[p] = qw1[tbl[SRC + p]]
+        qw2send[p] = qw1[tbl[SRC, p]]
         rows, cols = qw_place(me)
         to_peer(QW2, qw2send.at[p], qw2.at[rows, cols], p).start()
 
     each_peer(send_qw2)
     own_rows, own_cols = qw_place(me)
-    qw2[own_rows, own_cols] = qw1[tbl[SRC + me]]
+    qw2[own_rows, own_cols] = qw1[tbl[SRC, me]]
 
     each_peer(lambda p: to_peer(QH1, qh_part(p), qh1.at[me], p).start())
 
@@ -280,7 +311,7 @@
         wait_from(QW2, qw2.at[rows, cols], p)
 
     each_peer(wait_qw2)
-    idle = tbl[IDLE + me]
+    idle = tbl[IDLE, me]
     mine = pl.ds(pl.multiple_of(xl * 64, 64), 64)
     theirs = pl.ds(pl.multiple_of((1 - xl) * 64, 64), 64)
     Qw[z, mine, :] = jnp.where(idle > 0, qw2[...], qwown[...])
@@ -297,11 +328,11 @@
     hloc_cp.wait()
 
     def send_hidden(p):
-        hsend[p] = hloc[tbl[SIG + p]].reshape(NZ, PIECE, ROWS)
+        hsend[p] = hloc[tbl[SIG, p]].reshape(NZ, PIECE, ROWS)
         to_peer(HID, hsend.at[p], H.at[:, me], p).start()
 
     each_peer(send_hidden)
-    H[:, me] = hloc[tbl[SIG + me]].reshape(NZ, PIECE, ROWS)
+    H[:, me] = hloc[tbl[SIG, me]].reshape(NZ, PIECE, ROWS)
 
     pltpu.make_async_remote_copy(
         src_ref=Qw.at[z, theirs, :],
@@ -314,14 +345,12 @@
     ring_start(qpiece, qsem_s, qsem_r, 0)
 
     each_peer(lambda p: wait_from(VAL, vrecv.at[p], p))
-    v = vrecv[tbl[SRC + me]]
+    v = vrecv[tbl[SRC, me]].astype(F32)
     for c in range(8):
-        row, at = 3 + c // 2, 128 * (c % 2)
-        lw = jnp.broadcast_to(v[row : row + 1, at : at + 128], (128, 128)).T
+        lw = jnp.broadcast_to(v[6 + c : 7 + c, :], (128, 128)).T
         for r in range(6):
-            row, at = r // 2, 128 * (r % 2)
             DT[128 * c : 128 * (c + 1), 128 * r : 128 * (r + 1)] = 1.0 / (
-                lw * v[row : row + 1, at : at + 128] + damping_term
+                lw * v[r : r + 1, :] + damping_term
             )
 
     turn_width(z)
@@ -349,11 +378,11 @@
         return pl.ds(pl.multiple_of(p * SLAB, SLAB), SLAB)
 
     def send_qh2(p):
-        qh2send[p] = qh1[tbl[SRC + p]]
+        qh2send[p] = qh1[tbl[SRC, p]]
         to_peer(QH2, qh2send.at[p], Q.at[1, slab(me), :], p).start()
 
     each_peer(send_qh2)
-    Q[1, slab(me), :] = qh1[tbl[SRC + me]]
+    Q[1, slab(me), :] = qh1[tbl[SRC, me]]
 
     advance_q(0)
     advance_w(1)
@@ -375,11 +404,7 @@
     own_cp.wait()
     each_peer(lambda p: wait_from(QH2, Q.at[1, slab(p), :], p))
 
-    def left(n):
-        rows = pl.ds(pl.multiple_of(n * 256, 256), 256)
-        LT[rows, :] = jnp.dot(GT[rows, :], Q[idle], preferred_element_type=F32).astype(BF16)
-
-    each(BW // 256, left)
+    LT[...] = jnp.dot(GT[...], Q[idle], preferred_element_type=F32).astype(BF16)
     advance_q(3)
 
     def middle(n):
@@ -406,7 +431,8 @@
                 to_peer(OUT, res.at[q], R.at[me], q).start()
 
     each(4, finish)
-    R[me] = res[me]
+    mine_cp = pltpu.make_async_copy(res.at[me], R.at[me], loc.at[6])
+    mine_cp.start()
 
     each_peer(lambda p: wait_sent(WID, wsend.at[p], p))
     each_peer(lambda p: wait_sent(QW1, qw_part(p), p))
@@ -423,35 +449,38 @@
 
     each_peer(lambda p: wait_from(OUT, R.at[p], p))
     each_peer(lambda p: wait_sent(OUT, res.at[p], p))
-
-
-    def place(b):
-        out[b] = R[tbl[INV + b]]
-
-    each(N, place)
+    mine_cp.wait()
+
+
+def reorder(tbl, R, out, sem):
+    for b in range(N):
+        pltpu.make_async_copy(R.at[tbl[INV, b]], out.at[b], sem.at[b]).start()
+    for b in range(N):
+        pltpu.make_async_copy(R.at[0], out.at[b], sem.at[b]).wait()
 
 
 def body(
     width_side, hidden_side, block_owner, basis_hidden, basis_width, values_hidden, values_width
 ):
-    table = assignment(block_owner)
-    vals = jnp.concatenate(
-        [
-            values_hidden[0].astype(F32),
-            values_width[0].astype(F32),
-            jnp.zeros((2, 256), F32),
-        ],
-        axis=1,
-    ).reshape(2, 8, 256)
     any_spec = pl.BlockSpec(memory_space=pl.ANY)
     vmem_spec = pl.BlockSpec(memory_space=pltpu.VMEM)
     dma = pltpu.SemaphoreType.DMA
     smem_spec = pl.BlockSpec(memory_space=pltpu.SMEM)
-    return pl.pallas_call(
+    table, vals = pl.pallas_call(
+        prepare,
+        out_shape=(
+            jax.ShapeDtypeStruct((8, 128), jnp.int32),
+            jax.ShapeDtypeStruct((2, 16, 128), BF16),
+        ),
+        in_specs=[smem_spec, vmem_spec, vmem_spec],
+        out_specs=(vmem_spec, vmem_spec),
+        scratch_shapes=[pltpu.VMEM((2, 16, 128), F32)],
+    )(block_owner, values_hidden, values_width)
+    blocks = pl.pallas_call(
         kernel,
         out_shape=jax.ShapeDtypeStruct((N, SLAB, BW), BF16),
         in_specs=[smem_spec, vmem_spec] + [any_spec] * 4,
-        out_specs=vmem_spec,
+        out_specs=any_spec,
         scratch_shapes=[
             pltpu.VMEM((N, TOK, ROWS), BF16),
             pltpu.VMEM((N, PIECE, BW), BF16),
@@ -466,7 +495,7 @@
             pltpu.VMEM((64, BW), BF16),
             pltpu.VMEM((NZ, 128, BW), BF16),
             pltpu.VMEM((BW, BW), BF16),
-            pltpu.VMEM((N, 8, 256), F32),
+            pltpu.VMEM((N, 16, 128), BF16),
             pltpu.VMEM((N, SLAB, ROWS), BF16),
             pltpu.VMEM((N, SLAB, ROWS), BF16),
             pltpu.VMEM((2, ROWS, ROWS), BF16),
@@ -474,7 +503,6 @@
             pltpu.VMEM((BW, ROWS), BF16),
             pltpu.VMEM((BW, ROWS), F32),
             pltpu.VMEM((BW, ROWS), BF16),
-            pltpu.VMEM((N, SLAB, BW), BF16),
             pltpu.VMEM((N, SLAB, BW), BF16),
             dma((8, N)),
             dma((8, N)),
@@ -486,12 +514,20 @@
             dma((7,)),
         ],
         compiler_params=pltpu.CompilerParams(
-            collective_id=0, has_side_effects=True, vmem_limit_bytes=56 * 2**20
+            collective_id=0, has_side_effects=True, vmem_limit_bytes=51 * 2**20
         ),
         cost_estimate=pl.CostEstimate(
             flops=2 * ROWS * BW * (2048 + 2 * ROWS + 2 * BW), bytes_accessed=10 * 2**20, transcendentals=0
         ),
     )(table, vals, hidden_side, width_side, basis_hidden, basis_width)
+    return pl.pallas_call(
+        reorder,
+        out_shape=jax.ShapeDtypeStruct((N, SLAB, BW), BF16),
+        in_specs=[smem_spec, vmem_spec],
+        out_specs=any_spec,
+        scratch_shapes=[dma((N,))],
+        compiler_params=pltpu.CompilerParams(has_side_effects=True, vmem_limit_bytes=8 * 2**20),
+    )(table, blocks)
 
 
 def solution(mesh):

time: 128 us -> 123 us (0.961)
  other arithmetic: 4.68 us -> 0 us
    pallas_call x0 -> x2, Pallas kernels: none -> 3.3 us  [the longest x1 1.87 us: body(): pl.pallas_call(reorder, out_shape=jax.ShapeDtypeStruct((N, SLAB, BW), BF1...]
    pallas_call x1, Pallas kernels: 120 us -> 117 us  [body(): pl.pallas_call(kernel, out_shape=jax.ShapeDtypeStruct((N, SLAB, BW), BF16...]
    reduce_sum x3 -> x0, other arithmetic: 1.89 us -> none  [the longest x1 0.92 us: assignment(): slot = jnp.sum(jnp.logical_and(earlier, same).astype(jnp.int32), axis=1)]
    convert_element_type x2 -> x0, other arithmetic: 1.38 us -> none  [the longest x1 0.69 us: body(): values_width[0].astype(F32)]
    unnamed x2 -> x6, local copies, waits for them, and re-layouts: 3.32 us -> 2.32 us
where the time goes in v3:
time: 123 us
  Pallas kernels  121 us (98%)
  local copies, waits for them, and re-layouts  2.32 us (2%)
    pallas_call x1, Pallas kernels, body(): pl.pallas_call(kernel, out_shape=jax.ShapeDtypeStruct((N, SLAB, BW), BF16...  117 us

profile of v3, /device:TPU:1, one launch (start us, length us, event | category | flops | bytes accessed | tf_op | source)
XLA Modules:
  0.0 122.9 jit_solution(12457934285380694944)
XLA Ops:
  0.0 1.4 %shard_map.73 = (s32[8,128]{1,0:T(8,128)}, bf16[2,16,128]{2,1,0:T(8,128)(2,1)}) custom-call(s32[16]{0:T(128)} %owner.1, bf16[1,2,768]{2,1,0:T(2,128)(2,1)} %vh.1, bf16[1,2,1024]{2,1,0:T(2,128)(2,1)} %vw.1), custom_call_target="tpu_custom_call" | custom-call | tf_op jit(solution)/shard_map/pallas_call | solution.py:469
  1.4 0.0 copy-start
  1.4 0.7 copy-done
  2.1 0.0 copy-start.1
  2.1 0.9 copy-done.1
  3.1 0.0 copy-start.2
  3.1 0.7 copy-done.2
  3.8 117.2 %shard_map.74.R = bf16[16,48,1024]{2,1,0:T(8,128)(2,1)S(1)} custom-call(s32[8,128]{1,0:T(8,128)S(1)} %copy-done, bf16[2,16,128]{2,1,0:T(8,128)(2,1)S(1)} %copy-done.2, bf16[16,128,768]{2,1,0:T(8,128)(2,1)} %hid.1, bf16[16,128,1024]{2,1,0:T(8,128)(2,1)} %wid.1, bf16[1,2,768,768]{3,2,1,0:T(8,128)(2,1)} %qh.1, bf16[1,2,64,1024]{3,2,1,0:T(8,128)(2,1)S(1)} %copy-done.1), custom_call_target="tpu_custom_call" | custom-call | flops 8858370048 | bytes 10485760 | tf_op jit(solution)/shard_map/pallas_call | solution.py:479
  121.0 1.9 %shard_map.75 = bf16[16,48,1024]{2,1,0:T(8,128)(2,1)} custom-call(s32[8,128]{1,0:T(8,128)S(1)} %copy-done, bf16[16,48,1024]{2,1,0:T(8,128)(2,1)S(1)} %shard_map.74.R), custom_call_target="tpu_custom_call" | custom-call | tf_op jit(solution)/shard_map/pallas_call | solution.py:523
Async XLA Ops:
  1.4 0.7 copy-start
  2.1 0.9 copy-start.1
  3.1 0.7 copy-start.2

commit v4 on v3

--- a/solution.py
+++ b/solution.py
@@ -125,9 +125,9 @@
     side = z * 2 + (1 - xl)
 
     def peer(k):
-        y = lax.rem(me // 4 + k // 4, 4)
-        x = lax.rem((me // 2) % 2 + (k // 2) % 2, 2)
-        c = lax.rem(me % 2 + k % 2, 2)
+        y = lax.rem(me // 4 + k % 4, 4)
+        x = lax.rem((me // 2) % 2 + (k // 4) % 2, 2)
+        c = lax.rem(me % 2 + k // 8, 2)
         return y * 4 + x * 2 + c
 
     def each_peer(f):
@@ -208,64 +208,53 @@
     W[z, wrows(me), :] = wloc[tbl[SIG, me]]
     each_peer(lambda p: to_peer(VAL, vals.at[1], vrecv.at[me], p).start())
 
-    def wpiece(step, way):
-        if way == 0:
-            piece = lax.rem(z + NZ - step, NZ)
-        else:
-            piece = lax.rem(z + step, NZ)
-        if step < NZ // 2 - 1:
-            return W.at[piece]
-        half = N * PIECE // 2
-        return W.at[piece, pl.ds(way * half, half), :]
-
-    def qpiece(step, way):
-        if way == 0:
-            piece = lax.rem(z + NZ - step, NZ)
-        else:
-            piece = lax.rem(z + step, NZ)
-        if step < NZ // 2 - 1:
-            return Qw.at[piece]
-        return Qw.at[piece, pl.ds(way * 64, 64), :]
-
-    def ring(pieces, s, r, step, way):
-        part = pieces(step, way)
+    def piece_of(step, way):
+        return lax.rem(z + NZ - step, NZ) if way == 0 else lax.rem(z + step, NZ)
+
+    def travels(step, way, half):
+        return step < 3 or way == half
+
+    def wpart(step, way, half):
+        return W.at[piece_of(step, way), pl.ds(half * 128, 128), :]
+
+    def qpart(step, way, half):
+        return Qw.at[piece_of(step, way), pl.ds(half * 64, 64), :]
+
+    def ring(part, s, r, step, way, half):
         return pltpu.make_async_remote_copy(
             src_ref=part,
             dst_ref=part,
-            send_sem=s.at[way, step],
-            recv_sem=r.at[way, step],
+            send_sem=s.at[way, step, half],
+            recv_sem=r.at[way, step, half],
             device_id={"tensor": up if way == 0 else down},
             device_id_type=MESH,
         )
 
-    def landed(pieces, s, r, step, way):
-        part = pieces(step, way)
-        if way == 0:
-            piece = lax.rem(z + NZ - step - 1, NZ)
-        else:
-            piece = lax.rem(z + step + 1, NZ)
-        whole = W if pieces is wpiece else Qw
-        if step < NZ // 2 - 1:
-            part = whole.at[piece]
-        else:
-            half = (N * PIECE // 2) if pieces is wpiece else 64
-            part = whole.at[piece, pl.ds(way * half, half), :]
-        return pltpu.make_async_remote_copy(
-            src_ref=part,
-            dst_ref=part,
-            send_sem=s.at[way, step],
-            recv_sem=r.at[way, step],
-            device_id={"tensor": up if way == 0 else down},
-            device_id_type=MESH,
-        )
-
-    def ring_start(pieces, s, r, step):
+    def ring_start(parts, s, r, step, half):
         for way in range(2):
-            ring(pieces, s, r, step, way).start()
-
-    def ring_wait(pieces, s, r, step):
+            if travels(step, way, half):
+                ring(parts(step, way, half), s, r, step, way, half).start()
+
+    def ring_wait(parts, s, r, step, half):
         for way in range(2):
-            landed(pieces, s, r, step, way).wait_recv()
+            if travels(step, way, half):
+                ring(parts(step + 1, way, half), s, r, step, way, half).wait_recv()
+
+    def forward(parts, s, r, step):
+        for half in range(2):
+            ring_wait(parts, s, r, step, half)
+            if step < 3:
+                ring_start(parts, s, r, step + 1, half)
+
+    def ring_sent(parts, s, r):
+        for step in range(4):
+            for half in range(2):
+                for way in range(2):
+                    if travels(step, way, half):
+                        ring(parts(step, way, half), s, r, step, way, half).wait_send()
+
+    wring = (wpart, wsem_s, wsem_r)
+    qring = (qpart, qsem_s, qsem_r)
 
     def turn_width(piece):
         def part(n):
@@ -302,7 +291,8 @@
     each_peer(lambda p: to_peer(QH1, qh_part(p), qh1.at[me], p).start())
 
     each_peer(lambda p: wait_from(WID, W.at[z, wrows(p), :], p))
-    ring_start(wpiece, wsem_s, wsem_r, 0)
+    for half in range(2):
+        ring_start(*wring, 0, half)
 
     qwown_cp.wait()
 
@@ -334,6 +324,7 @@
     each_peer(send_hidden)
     H[:, me] = hloc[tbl[SIG, me]].reshape(NZ, PIECE, ROWS)
 
+    forward(*wring, 0)
     pltpu.make_async_remote_copy(
         src_ref=Qw.at[z, theirs, :],
         dst_ref=Qw.at[z, theirs, :],
@@ -342,7 +333,10 @@
         device_id={"tensor": side},
         device_id_type=MESH,
     ).wait_recv()
-    ring_start(qpiece, qsem_s, qsem_r, 0)
+    for half in range(2):
+        ring_start(*qring, 0, half)
+    turn_width(z)
+    turn_basis(z)
 
     each_peer(lambda p: wait_from(VAL, vrecv.at[p], p))
     v = vrecv[tbl[SRC, me]].astype(F32)
@@ -353,23 +347,11 @@
                 lw * v[r : r + 1, :] + damping_term
             )
 
-    turn_width(z)
-    turn_basis(z)
-
-    def advance(pieces, s, r, step, turn):
-        ring_wait(pieces, s, r, step)
-        if step < 3:
-            ring_start(pieces, s, r, step + 1)
-        for piece in ((z + NZ - step - 1) % NZ, (z + step + 1) % NZ)[: 2 if step < 3 else 1]:
-            turn(piece)
-
-    def advance_w(step):
-        advance(wpiece, wsem_s, wsem_r, step, turn_width)
-
-    def advance_q(step):
-        advance(qpiece, qsem_s, qsem_r, step, turn_basis)
-
-    advance_w(0)
+    def turn(one, step):
+        for way in range(2 if step < 3 else 1):
+            one(piece_of(step + 1, way))
+
+    turn(turn_width, 0)
 
     qh1_cp.wait()
     each_peer(lambda p: wait_from(QH1, qh1.at[p], p))
@@ -384,36 +366,32 @@
     each_peer(send_qh2)
     Q[1, slab(me), :] = qh1[tbl[SRC, me]]
 
-    advance_q(0)
-    advance_w(1)
-    advance_q(1)
-    advance_w(2)
-    advance_q(2)
-    advance_w(3)
+    forward(*qring, 0)
+    forward(*wring, 1)
+    turn(turn_basis, 0)
+    turn(turn_width, 1)
+    forward(*qring, 1)
+    forward(*wring, 2)
+    turn(turn_basis, 1)
+    turn(turn_width, 2)
+    forward(*qring, 2)
+    forward(*wring, 3)
+    turn(turn_basis, 2)
+    turn(turn_width, 3)
 
     each_peer(lambda p: wait_from(HID, H.at[:, p], p))
 
-    def gradient(n):
-        rows = pl.ds(pl.multiple_of(n * 256, 256), 256)
-        GT[rows, :] = jnp.dot(
-            WT[rows, :], H[...].reshape(N * TOK, ROWS), preferred_element_type=F32
-        ).astype(BF16)
-
-    each(BW // 256, gradient)
+    GT[...] = jnp.dot(
+        WT[...], H[...].reshape(N * TOK, ROWS), preferred_element_type=F32
+    ).astype(BF16)
 
     own_cp.wait()
     each_peer(lambda p: wait_from(QH2, Q.at[1, slab(p), :], p))
 
     LT[...] = jnp.dot(GT[...], Q[idle], preferred_element_type=F32).astype(BF16)
-    advance_q(3)
-
-    def middle(n):
-        rows = pl.ds(pl.multiple_of(n * 256, 256), 256)
-        S[rows, :] = (
-            jnp.dot(QwT[rows, :], LT[...], preferred_element_type=F32) * DT[rows, :]
-        ).astype(BF16)
-
-    each(BW // 256, middle)
+    forward(*qring, 3)
+    turn(turn_basis, 3)
+    S[...] = (jnp.dot(QwT[...], LT[...], preferred_element_type=F32) * DT[...]).astype(BF16)
 
     def finish(n):
         group = lax.rem(me // 4 + 1 + n, 4)
@@ -442,21 +420,22 @@
     each_peer(lambda p: wait_sent(HID, hsend.at[p], p))
     each_peer(lambda p: wait_sent(QH2, qh2send.at[p], p))
     swap.wait_send()
-    for step in range(4):
-        for way in range(2):
-            ring(wpiece, wsem_s, wsem_r, step, way).wait_send()
-            ring(qpiece, qsem_s, qsem_r, step, way).wait_send()
+    ring_sent(*wring)
+    ring_sent(*qring)
 
     each_peer(lambda p: wait_from(OUT, R.at[p], p))
     each_peer(lambda p: wait_sent(OUT, res.at[p], p))
     mine_cp.wait()
 
 
-def reorder(tbl, R, out, sem):
+def reorder(tbl, R, out, held, in_sem, out_sem):
     for b in range(N):
-        pltpu.make_async_copy(R.at[tbl[INV, b]], out.at[b], sem.at[b]).start()
+        pltpu.make_async_copy(R.at[tbl[INV, b]], held.at[b], in_sem.at[b]).start()
     for b in range(N):
-        pltpu.make_async_copy(R.at[0], out.at[b], sem.at[b]).wait()
+        pltpu.make_async_copy(R.at[0], held.at[b], in_sem.at[b]).wait()
+        pltpu.make_async_copy(held.at[b], out.at[b], out_sem.at[b]).start()
+    for b in range(N):
+        pltpu.make_async_copy(held.at[b], out.at[b], out_sem.at[b]).wait()
 
 
 def body(
@@ -475,6 +454,7 @@
         in_specs=[smem_spec, vmem_spec, vmem_spec],
         out_specs=(vmem_spec, vmem_spec),
         scratch_shapes=[pltpu.VMEM((2, 16, 128), F32)],
+        compiler_params=pltpu.CompilerParams(vmem_limit_bytes=60 * 2**20),
     )(block_owner, values_hidden, values_width)
     blocks = pl.pallas_call(
         kernel,
@@ -506,15 +486,15 @@
             pltpu.VMEM((N, SLAB, BW), BF16),
             dma((8, N)),
             dma((8, N)),
-            dma((2, 4)),
-            dma((2, 4)),
-            dma((2, 4)),
-            dma((2, 4)),
+            dma((2, 4, 2)),
+            dma((2, 4, 2)),
+            dma((2, 4, 2)),
+            dma((2, 4, 2)),
             dma((2,)),
             dma((7,)),
         ],
         compiler_params=pltpu.CompilerParams(
-            collective_id=0, has_side_effects=True, vmem_limit_bytes=51 * 2**20
+            collective_id=0, has_side_effects=True, vmem_limit_bytes=60 * 2**20
         ),
         cost_estimate=pl.CostEstimate(
             flops=2 * ROWS * BW * (2048 + 2 * ROWS + 2 * BW), bytes_accessed=10 * 2**20, transcendentals=0
@@ -523,10 +503,10 @@
     return pl.pallas_call(
         reorder,
         out_shape=jax.ShapeDtypeStruct((N, SLAB, BW), BF16),
-        in_specs=[smem_spec, vmem_spec],
+        in_specs=[smem_spec, any_spec],
         out_specs=any_spec,
-        scratch_shapes=[dma((N,))],
-        compiler_params=pltpu.CompilerParams(has_side_effects=True, vmem_limit_bytes=8 * 2**20),
+        scratch_shapes=[pltpu.VMEM((N, SLAB, BW), BF16), dma((N,)), dma((N,))],
+        compiler_params=pltpu.CompilerParams(has_side_effects=True, vmem_limit_bytes=60 * 2**20),
     )(table, blocks)
 
 

time: 123 us -> 121 us (0.984)
  local copies, waits for them, and re-layouts: 2.32 us -> 0 us
    unnamed x6 -> x0, local copies, waits for them, and re-layouts: 2.32 us -> none
    pallas_call x1, Pallas kernels: 1.87 us -> 3.12 us  [body(): pl.pallas_call(reorder, out_shape=jax.ShapeDtypeStruct((N, SLAB, BW), BF1...]
where the time goes in v4:
time: 121 us
  Pallas kernels  121 us (100%)
    pallas_call x1, Pallas kernels, body(): pl.pallas_call(kernel, out_shape=jax.ShapeDtypeStruct((N, SLAB, BW), BF16...  116 us
    pallas_call x1, Pallas kernels, body(): pl.pallas_call(reorder, out_shape=jax.ShapeDtypeStruct((N, SLAB, BW), BF1...  3.12 us

profile of v4, /device:TPU:1, one launch (start us, length us, event | category | flops | bytes accessed | tf_op | source)
XLA Modules:
  0.0 120.7 jit_solution(8012411354828101910)
XLA Ops:
  0.0 1.4 %shard_map.73 = (s32[8,128]{1,0:T(8,128)}, bf16[2,16,128]{2,1,0:T(8,128)(2,1)}) custom-call(s32[16]{0:T(128)} %owner.1, bf16[1,2,768]{2,1,0:T(2,128)(2,1)} %vh.1, bf16[1,2,1024]{2,1,0:T(2,128)(2,1)} %vw.1), custom_call_target="tpu_custom_call" | custom-call | tf_op jit(solution)/shard_map/pallas_call | solution.py:448
  1.4 116.1 %shard_map.74.R = bf16[16,48,1024]{2,1,0:T(8,128)(2,1)} custom-call(s32[8,128]{1,0:T(8,128)} %get-tuple-element.7.tbl, bf16[2,16,128]{2,1,0:T(8,128)(2,1)} %get-tuple-element.8.vals, bf16[16,128,768]{2,1,0:T(8,128)(2,1)} %hid.1, bf16[16,128,1024]{2,1,0:T(8,128)(2,1)} %wid.1, bf16[1,2,768,768]{3,2,1,0:T(8,128)(2,1)} %qh.1, bf16[1,2,64,1024]{3,2,1,0:T(8,128)(2,1)} %qw.1), custom_call_target="tpu_custom_call" | custom-call | flops 8858370048 | bytes 10485760 | tf_op jit(solution)/shard_map/pallas_call | solution.py:459
  117.6 3.1 %shard_map.75 = bf16[16,48,1024]{2,1,0:T(8,128)(2,1)} custom-call(s32[8,128]{1,0:T(8,128)} %get-tuple-element.7.tbl, bf16[16,48,1024]{2,1,0:T(8,128)(2,1)} %shard_map.74.R), custom_call_target="tpu_custom_call" | custom-call | tf_op jit(solution)/shard_map/pallas_call | solution.py:503

commit v5 on v4

--- a/solution.py
+++ b/solution.py
@@ -103,6 +103,7 @@
     qh1,
     qh2send,
     Q,
+    acc,
     GT,
     LT,
     DT,
@@ -256,12 +257,19 @@
     wring = (wpart, wsem_s, wsem_r)
     qring = (qpart, qsem_s, qsem_r)
 
-    def turn_width(piece):
+    places = (0, 1, 2, 3, 5, 6, 7, 4)
+
+    def turn_width(piece, away=0):
+        at = 256 * places.index(away)
+
         def part(n):
             cols = pl.ds(pl.multiple_of(n * 256, 256), 256)
-            WT[cols, pl.ds(pl.multiple_of(piece * 256, 256), 256)] = W[piece, :, cols].T
+            WT[cols, at : at + 256] = W[piece, :, cols].T
 
         each(BW // 256, part)
+
+    def tokens(away):
+        return H[lax.rem(z + away, NZ)].reshape(N * PIECE, ROWS)
 
     def turn_basis(piece):
         def part(n):
@@ -349,7 +357,11 @@
 
     def turn(one, step):
         for way in range(2 if step < 3 else 1):
-            one(piece_of(step + 1, way))
+            piece = piece_of(step + 1, way)
+            if one is turn_width:
+                one(piece, NZ - step - 1 if way == 0 else step + 1)
+            else:
+                one(piece)
 
     turn(turn_width, 0)
 
@@ -375,15 +387,16 @@
     turn(turn_basis, 1)
     turn(turn_width, 2)
     forward(*qring, 2)
+
+    each_peer(lambda p: wait_from(HID, H.at[:, p], p))
+    most = jnp.concatenate([tokens(away) for away in places[:7]], axis=0)
+    acc[...] = jnp.dot(WT[:, : 7 * 256], most, preferred_element_type=F32)
     forward(*wring, 3)
+    turn(turn_width, 3)
+    GT[...] = (
+        acc[...] + jnp.dot(WT[:, 7 * 256 :], tokens(4), preferred_element_type=F32)
+    ).astype(BF16)
     turn(turn_basis, 2)
-    turn(turn_width, 3)
-
-    each_peer(lambda p: wait_from(HID, H.at[:, p], p))
-
-    GT[...] = jnp.dot(
-        WT[...], H[...].reshape(N * TOK, ROWS), preferred_element_type=F32
-    ).astype(BF16)
 
     own_cp.wait()
     each_peer(lambda p: wait_from(QH2, Q.at[1, slab(p), :], p))
@@ -479,6 +492,7 @@
             pltpu.VMEM((N, SLAB, ROWS), BF16),
             pltpu.VMEM((N, SLAB, ROWS), BF16),
             pltpu.VMEM((2, ROWS, ROWS), BF16),
+            pltpu.VMEM((BW, ROWS), F32),
             pltpu.VMEM((BW, ROWS), BF16),
             pltpu.VMEM((BW, ROWS), BF16),
             pltpu.VMEM((BW, ROWS), F32),

time: 121 us -> 120 us (level)
  Pallas kernels: 121 us -> 119 us
    pallas_call x1, Pallas kernels: 116 us -> 115 us  [body(): pl.pallas_call(kernel, out_shape=jax.ShapeDtypeStruct((N, SLAB, BW), BF16...]
where the time goes in v5:
time: 120 us; the launch traced here: 119 us
  Pallas kernels  119 us (99%)
    pallas_call x1, Pallas kernels, body(): pl.pallas_call(kernel, out_shape=jax.ShapeDtypeStruct((N, SLAB, BW), BF16...  115 us
    pallas_call x1, Pallas kernels, body(): pl.pallas_call(reorder, out_shape=jax.ShapeDtypeStruct((N, SLAB, BW), BF1...  3.12 us

profile of v5, /device:TPU:1, one launch (start us, length us, event | category | flops | bytes accessed | tf_op | source)
XLA Modules:
  0.0 119.3 jit_solution(15519059220458060380)
XLA Ops:
  0.0 1.4 %shard_map.73 = (s32[8,128]{1,0:T(8,128)}, bf16[2,16,128]{2,1,0:T(8,128)(2,1)}) custom-call(s32[16]{0:T(128)} %owner.1, bf16[1,2,768]{2,1,0:T(2,128)(2,1)} %vh.1, bf16[1,2,1024]{2,1,0:T(2,128)(2,1)} %vw.1), custom_call_target="tpu_custom_call" | custom-call | tf_op jit(solution)/shard_map/pallas_call | solution.py:461
  1.4 114.7 %shard_map.74.R = bf16[16,48,1024]{2,1,0:T(8,128)(2,1)} custom-call(s32[8,128]{1,0:T(8,128)} %get-tuple-element.7.tbl, bf16[2,16,128]{2,1,0:T(8,128)(2,1)} %get-tuple-element.8.vals, bf16[16,128,768]{2,1,0:T(8,128)(2,1)} %hid.1, bf16[16,128,1024]{2,1,0:T(8,128)(2,1)} %wid.1, bf16[1,2,768,768]{3,2,1,0:T(8,128)(2,1)} %qh.1, bf16[1,2,64,1024]{3,2,1,0:T(8,128)(2,1)} %qw.1), custom_call_target="tpu_custom_call" | custom-call | flops 8858370048 | bytes 10485760 | tf_op jit(solution)/shard_map/pallas_call | solution.py:472
  116.2 3.1 %shard_map.75 = bf16[16,48,1024]{2,1,0:T(8,128)(2,1)} custom-call(s32[8,128]{1,0:T(8,128)} %get-tuple-element.7.tbl, bf16[16,48,1024]{2,1,0:T(8,128)(2,1)} %shard_map.74.R), custom_call_target="tpu_custom_call" | custom-call | tf_op jit(solution)/shard_map/pallas_call | solution.py:517

commit v6 on v5

--- a/solution.py
+++ b/solution.py
@@ -296,7 +296,7 @@
     own_rows, own_cols = qw_place(me)
     qw2[own_rows, own_cols] = qw1[tbl[SRC, me]]
 
-    each_peer(lambda p: to_peer(QH1, qh_part(p), qh1.at[me], p).start())
+    lax.fori_loop(1, 8, lambda k, _: (to_peer(QH1, qh_part(peer(k)), qh1.at[me], peer(k)).start(), None)[1], None)
 
     each_peer(lambda p: wait_from(WID, W.at[z, wrows(p), :], p))
     for half in range(2):
@@ -322,6 +322,7 @@
         device_id_type=MESH,
     )
     swap.start()
+    lax.fori_loop(8, N, lambda k, _: (to_peer(QH1, qh_part(peer(k)), qh1.at[me], peer(k)).start(), None)[1], None)
 
     hloc_cp.wait()
 

time: 120 us -> 120 us (level)
  no operation moved by 1% of the time
where the time goes in v6:
time: 120 us; the launch traced here: 119 us
  Pallas kernels  119 us (99%)
    pallas_call x1, Pallas kernels, body(): pl.pallas_call(kernel, out_shape=jax.ShapeDtypeStruct((N, SLAB, BW), BF16...  115 us
    pallas_call x1, Pallas kernels, body(): pl.pallas_call(reorder, out_shape=jax.ShapeDtypeStruct((N, SLAB, BW), BF1...  3.12 us

profile of v6, /device:TPU:1, one launch (start us, length us, event | category | flops | bytes accessed | tf_op | source)
XLA Modules:
  0.0 119.3 jit_solution(4764370299433695896)
XLA Ops:
  0.0 1.4 %shard_map.73 = (s32[8,128]{1,0:T(8,128)}, bf16[2,16,128]{2,1,0:T(8,128)(2,1)}) custom-call(s32[16]{0:T(128)} %owner.1, bf16[1,2,768]{2,1,0:T(2,128)(2,1)} %vh.1, bf16[1,2,1024]{2,1,0:T(2,128)(2,1)} %vw.1), custom_call_target="tpu_custom_call" | custom-call | tf_op jit(solution)/shard_map/pallas_call | solution.py:462
  1.4 114.7 %shard_map.74.R = bf16[16,48,1024]{2,1,0:T(8,128)(2,1)} custom-call(s32[8,128]{1,0:T(8,128)} %get-tuple-element.7.tbl, bf16[2,16,128]{2,1,0:T(8,128)(2,1)} %get-tuple-element.8.vals, bf16[16,128,768]{2,1,0:T(8,128)(2,1)} %hid.1, bf16[16,128,1024]{2,1,0:T(8,128)(2,1)} %wid.1, bf16[1,2,768,768]{3,2,1,0:T(8,128)(2,1)} %qh.1, bf16[1,2,64,1024]{3,2,1,0:T(8,128)(2,1)} %qw.1), custom_call_target="tpu_custom_call" | custom-call | flops 8858370048 | bytes 10485760 | tf_op jit(solution)/shard_map/pallas_call | solution.py:473
  116.2 3.1 %shard_map.75 = bf16[16,48,1024]{2,1,0:T(8,128)(2,1)} custom-call(s32[8,128]{1,0:T(8,128)} %get-tuple-element.7.tbl, bf16[16,48,1024]{2,1,0:T(8,128)(2,1)} %shard_map.74.R), custom_call_target="tpu_custom_call" | custom-call | tf_op jit(solution)/shard_map/pallas_call | solution.py:518
